TPU v7x, 32 devices: a whole 2x2x4 slice. The times are simulated.
32 devices in a mesh: seq: 4 (over y, x), head: 8 (over z, core).
Axes of the slice: x: 2, y: 2, z: 4, core: 2. Of those that a mesh axis runs over, the one named last changes fastest.
Arguments:
- queries: bfloat16 [8192, 4096], P('seq', 'head'), may hold values from -80 to 80
- transposed_keys: bfloat16 [512, 8192], P('head', 'seq'), may hold values from -25 to 25
- transposed_values: bfloat16 [512, 8192], P('head', 'seq'), may hold values from -6 to 6
- adapter_down_factor: bfloat16 [4096, 64], P('head'), may hold values from -0.5 to 0.5
- adapter_up_factor: bfloat16 [64, 4096], P(None, 'head'), may hold values from -0.75 to 0.75
- projection_output_gradient: bfloat16 [8192, 4096], P('seq', 'head'), may hold values from -0.0625 to 0.0625
Outputs:
- adapter_activations: float32 [64, 8192], P(None, 'seq')
- down_factor_gradient: float32 [4096, 64], P('head')
- up_factor_gradient: float32 [64, 4096], P(None, 'head')
All inputs are finite; a program needn't handle non-finite values.
Results may differ from a plain program's by a relative error of at most 0.0046.
Values may be sent and summed in bfloat16 or wider, within the bound.
A program may use at most 64 MiB of HBM per device.

v0:
```python
import functools
import math

import jax
import jax.numpy as jnp
from jax import lax
from jax.experimental import pallas as pl
from jax.experimental.pallas import tpu as pltpu
from jax.sharding import PartitionSpec as P

neg_big = -1e30
adapter_scale = 2.0
head_size = 128
block = 512
sum_type = jnp.bfloat16
NT = (((1,), (1,)), ((), ()))
TN = (((0,), (0,)), ((), ()))


def pieces_of(rows, columns, count):
    across = min(count, columns // 128)
    down = count // across
    return rows // down, columns // across, across


def kernel(
    n_seq,
    n_head,
    q_hbm,
    k_hbm,
    v_hbm,
    down_ref,
    up_ref,
    grad_hbm,
    act_out,
    down_out,
    up_out,
    q_ref,
    grad_ref,
    k_ref,
    v_ref,
    kt_ref,
    attn_ref,
    back_pair,
    back_pair_in,
    back_send,
    back_in,
    back_all,
    back_ref,
    act_pair,
    act_pair_in,
    act_send,
    act_in,
    act_all,
    low_ref,
    seq_send,
    seq_in,
    seq_all,
    local_sem,
    kv_send,
    kv_in,
    pair_send_sem,
    pair_in_sem,
    rs_send_sem,
    rs_in_sem,
    ag_send_sem,
    ag_in_sem,
    seq_send_sem,
    seq_in_sem,
):
    me_s, me_h = lax.axis_index("seq"), lax.axis_index("head")
    n_chip = n_head // 2
    chip, core = me_h // 2, me_h % 2
    partner = {"head": me_h + 1 - 2 * core}
    sh = 1 - me_h // (n_head // 2)
    length = q_ref.shape[0]
    half = length // 2
    n_local = q_ref.shape[1] // head_size
    rank = up_ref.shape[0]
    mid = rank // 2
    own = k_hbm.shape[0]
    n_block = length // block
    pr, pc, across = pieces_of(mid, block, n_chip)
    sr, sc, s_across = pieces_of(rank, block, n_seq)

    def piece(value, index):
        r, c = (index // across) * pr, (index % across) * pc
        return value[r : r + pr, c : c + pc]

    def remote(src, dst, send, recv, device):
        copy = pltpu.make_async_remote_copy(
            src_ref=src,
            dst_ref=dst,
            send_sem=send,
            recv_sem=recv,
            device_id=device,
            device_id_type=pl.DeviceIdType.MESH,
        )
        copy.start()
        return copy

    def settle(ref, sem):
        pltpu.make_async_copy(ref, ref, sem).wait()

    barrier = pltpu.get_barrier_semaphore()
    for step in range(1, n_head):
        pl.semaphore_signal(
            barrier,
            inc=1,
            device_id={"head": lax.rem(me_h + step, n_head)},
            device_id_type=pl.DeviceIdType.MESH,
        )
    for step in range(1, n_seq):
        pl.semaphore_signal(
            barrier,
            inc=1,
            device_id={"seq": lax.rem(me_s + step, n_seq)},
            device_id_type=pl.DeviceIdType.MESH,
        )

    own_rows = pl.ds(pl.multiple_of(core * own, own), own)
    grad_copy = pltpu.make_async_copy(grad_hbm, grad_ref, local_sem.at[0])
    k_copy = pltpu.make_async_copy(k_hbm, k_ref.at[own_rows, pl.ds(half, length)], local_sem.at[1])
    v_copy = pltpu.make_async_copy(v_hbm, v_ref.at[own_rows, pl.ds(half, length)], local_sem.at[2])
    q_copy = pltpu.make_async_copy(q_hbm, q_ref, local_sem.at[3])
    for copy in (grad_copy, k_copy, v_copy, q_copy):
        copy.start()

    grad_copy.wait()
    for b in range(n_block):
        part = lax.dot_general(
            up_ref[...],
            grad_ref[b * block : (b + 1) * block, :],
            NT,
            preferred_element_type=jnp.float32,
        )
        back_pair[0, b] = part[:mid]
        back_pair[1, b] = part[mid:]
    pl.semaphore_wait(barrier, n_head + n_seq - 2)

    kv_copies = []
    for i, (src, dst) in enumerate(((k_hbm, k_ref), (v_hbm, v_ref))):
        kv_copies.append(
            remote(
                src,
                dst.at[own_rows, pl.ds(half, length)],
                kv_send.at[i],
                kv_in.at[i],
                partner,
            )
        )

    def tail_copy(i, src, dst):
        return pltpu.make_async_remote_copy(
            src_ref=src.at[:, pl.ds(half, half)],
            dst_ref=dst.at[own_rows, pl.ds(0, half)],
            send_sem=kv_send.at[2 + i],
            recv_sem=kv_in.at[2 + i],
            device_id={"seq": lax.rem(me_s + 1, n_seq)},
            device_id_type=pl.DeviceIdType.MESH,
        )

    def forward_copy(i, ref):
        return pltpu.make_async_remote_copy(
            src_ref=ref.at[own_rows, pl.ds(0, half)],
            dst_ref=ref.at[own_rows, pl.ds(0, half)],
            send_sem=kv_send.at[4 + i],
            recv_sem=kv_in.at[4 + i],
            device_id=partner,
            device_id_type=pl.DeviceIdType.MESH,
        )

    tails = [tail_copy(0, k_hbm, k_ref), tail_copy(1, v_hbm, v_ref)]
    forwards = [forward_copy(0, k_ref), forward_copy(1, v_ref)]

    @pl.when(sh == 1)
    def _():
        for copy in tails:
            copy.start()

    back_pair_copy = remote(
        back_pair.at[1 - core],
        back_pair_in,
        pair_send_sem.at[n_block],
        pair_in_sem.at[n_block],
        partner,
    )

    for copy in (k_copy, v_copy, q_copy):
        copy.wait()
    kv_copies[0].wait_recv()
    kv_copies[1].wait_recv()
    for c in range(half, half + length, block):
        kt_ref[c : c + block, :] = k_ref[:, c : c + block].T

    def peers():
        for step in range(1, n_chip):
            yield lax.rem(chip + step, n_chip)

    def back_scatter():
        back_pair_copy.wait_recv()
        for b in range(n_block):
            total = back_pair[core, b] + back_pair_in[b]
            for p in range(n_chip):
                back_send[p, b] = piece(total, p).astype(sum_type)
        back_in[chip] = back_send[chip]
        for peer in peers():
            remote(
                back_send.at[peer],
                back_in.at[chip],
                rs_send_sem.at[n_block],
                rs_in_sem.at[n_block],
                {"head": peer * 2 + core},
            )

    def gather_send(buffer, index):
        for step in range(1, n_head):
            remote(
                buffer.at[me_h],
                buffer.at[me_h],
                ag_send_sem.at[index],
                ag_in_sem.at[index],
                {"head": lax.rem(me_h + step, n_head)},
            )

    def back_gather():
        settle(back_in.at[pl.ds(0, n_chip - 1)], rs_in_sem.at[n_block])
        total = back_in[0].astype(jnp.float32)
        for p in range(1, n_chip):
            total = total + back_in[p].astype(jnp.float32)
        back_all[me_h] = total.astype(jnp.bfloat16)
        gather_send(back_all, 2)

    def place(d):
        r = (d % 2) * mid + ((d // 2) // across) * pr
        c = ((d // 2) % across) * pc
        return r, c

    def back_finish():
        settle(back_all.at[pl.ds(0, n_head - 1)], ag_in_sem.at[2])
        for d in range(n_head):
            r, c = place(d)
            for b in range(n_block):
                back_ref[r : r + pr, b * block + c : b * block + c + pc] = back_all[d, b]

    def block_of(n):
        return lax.rem(n - 1 + sh * (n_block // 2), n_block)

    def act_part(n):
        b = block_of(n)
        columns = pl.ds(pl.multiple_of(b * block, block), block)
        part = lax.dot_general(
            down_ref[...], attn_ref[:, columns], TN, preferred_element_type=jnp.float32
        )
        act_pair[n - 1, 0] = part[:mid]
        act_pair[n - 1, 1] = part[mid:]
        return remote(
            act_pair.at[n - 1, 1 - core],
            act_pair_in.at[n - 1],
            pair_send_sem.at[n - 1],
            pair_in_sem.at[n - 1],
            partner,
        )

    def act_scatter(n, copy):
        b = block_of(n)
        copy.wait_recv()
        total = act_pair[n - 1, core] + act_pair_in[n - 1]
        for p in range(n_chip):
            act_send[n - 1, p] = piece(total, p).astype(sum_type)
        act_in[b, chip] = act_send[n - 1, chip]
        for peer in peers():
            remote(
                act_send.at[n - 1, peer],
                act_in.at[b, chip],
                rs_send_sem.at[n - 1],
                rs_in_sem.at[b],
                {"head": peer * 2 + core},
            )

    def act_gather(odd):
        for i, b in enumerate(range(odd, n_block, 2)):
            settle(act_in.at[b, pl.ds(0, n_chip - 1)], rs_in_sem.at[b])
            total = act_in[b, 0].astype(jnp.float32)
            for p in range(1, n_chip):
                total = total + act_in[b, p].astype(jnp.float32)
            act_all[odd, me_h, i] = total.astype(jnp.bfloat16)
        gather_send(act_all.at[odd], odd)

    def act_finish(odd):
        settle(act_all.at[odd, pl.ds(0, n_head - 1)], ag_in_sem.at[odd])
        for d in range(n_head):
            r, c = place(d)
            for i, b in enumerate(range(odd, n_block, 2)):
                value = act_all[odd, d, i]
                low_ref[r : r + pr, b * block + c : b * block + c + pc] = value
                act_out[r : r + pr, b * block + c : b * block + c + pc] = value.astype(jnp.float32)

    def up_part(odd):
        total = None
        for b in range(odd, n_block, 2):
            term = jnp.dot(
                low_ref[:, b * block : (b + 1) * block],
                grad_ref[b * block : (b + 1) * block, :],
                preferred_element_type=jnp.float32,
            )
            total = term if total is None else total + term
        return total

    sub = block // 2
    factor = math.log2(math.e) / math.sqrt(head_size)

    def attend(n, hooks):
        b = block_of(n)
        shifted_start = length if n <= n_block // 2 else 0
        start = pl.multiple_of(half + sh * (shifted_start - half), half)

        def body(h, carry):
            for at, hook in hooks:
                pl.when(h == at)(hook)
            columns = pl.ds(pl.multiple_of(h * head_size, head_size), head_size)
            for r in range(2):
                rows = pl.ds(pl.multiple_of(b * block + r * sub, sub), sub)
                query = q_ref[rows, columns]
                count = (n - 1) * 2 + r + 1
                scores = []
                for j in range(count):
                    keys = kt_ref[pl.ds(pl.multiple_of(start + j * sub, sub), sub), :]
                    score = lax.dot_general(keys, query, NT, preferred_element_type=jnp.float32)
                    if j == count - 1:
                        key_index = lax.broadcasted_iota(jnp.int32, score.shape, 0)
                        row_index = lax.broadcasted_iota(jnp.int32, score.shape, 1)
                        score = jnp.where(key_index <= row_index, score, neg_big)
                    scores.append(score)
                top = jnp.max(scores[0], axis=0, keepdims=True)
                for score in scores[1:]:
                    top = jnp.maximum(top, jnp.max(score, axis=0, keepdims=True))
                total, context = None, None
                for j in range(count):
                    weights = jnp.exp2((scores[j] - top) * factor)
                    row_sum = jnp.sum(weights, axis=0, keepdims=True)
                    values = v_ref[:, pl.ds(pl.multiple_of(start + j * sub, sub), sub)]
                    term = jnp.dot(
                        values, weights.astype(jnp.bfloat16), preferred_element_type=jnp.float32
                    )
                    total = row_sum if total is None else total + row_sum
                    context = term if context is None else context + term
                attn_ref[columns, rows] = (context * (1.0 / total)).astype(jnp.bfloat16)
            return carry

        lax.fori_loop(0, n_local, body, 0)

    pairs = {}
    attend(2, [(1, back_scatter)])
    pairs[2] = act_part(2)

    @pl.when(sh == 1)
    def _():
        for tail, forward in zip(tails, forwards):
            tail.wait_recv()
            forward.start()

    attend(1, [])
    pairs[1] = act_part(1)

    @pl.when(sh == 1)
    def _():
        for copy in forwards:
            copy.wait_recv()
        for c in range(0, half, block):
            kt_ref[c : c + block, :] = k_ref[:, c : c + block].T

    def early():
        act_scatter(2, pairs[2])
        act_scatter(1, pairs[1])
        back_gather()

    attend(4, [(1, early)])
    pairs[4] = act_part(4)

    def late():
        act_scatter(4, pairs[4])
        back_finish()

    attend(3, [(1, late), (3, functools.partial(act_gather, 1))])
    pairs[3] = act_part(3)

    def seq_scatter(kind, value):
        for p in range(n_seq):
            r, c = (p // s_across) * sr, (p % s_across) * sc
            seq_send[kind, p] = value[r : r + sr, c : c + sc]
        seq_in[kind, me_s] = seq_send[kind, me_s]
        for step in range(1, n_seq):
            peer = lax.rem(me_s + step, n_seq)
            remote(
                seq_send.at[kind, peer],
                seq_in.at[kind, me_s],
                seq_send_sem.at[kind, 0],
                seq_in_sem.at[kind, 0],
                {"seq": peer},
            )

    def seq_gather(kind):
        settle(seq_in.at[kind, pl.ds(0, n_seq - 1)], seq_in_sem.at[kind, 0])
        total = seq_in[kind, 0]
        for p in range(1, n_seq):
            total = total + seq_in[kind, p]
        seq_all[kind, me_s] = total * adapter_scale
        for step in range(1, n_seq):
            remote(
                seq_all.at[kind, me_s],
                seq_all.at[kind, me_s],
                seq_send_sem.at[kind, 1],
                seq_in_sem.at[kind, 1],
                {"seq": lax.rem(me_s + step, n_seq)},
            )

    act_finish(1)
    up_total = up_part(1)
    act_scatter(3, pairs[3])
    seq_scatter(
        0,
        lax.dot_general(back_ref[...], attn_ref[...], NT, preferred_element_type=jnp.float32),
    )
    act_gather(0)
    seq_gather(0)
    act_finish(0)
    seq_scatter(1, up_total + up_part(0))

    settle(seq_all.at[0, pl.ds(0, n_seq - 1)], seq_in_sem.at[0, 1])
    for p in range(n_seq):
        r, c = (p // s_across) * sr, (p % s_across) * sc
        down_out[c : c + sc, r : r + sr] = seq_all[0, p].T
    seq_gather(1)
    settle(seq_all.at[1, pl.ds(0, n_seq - 1)], seq_in_sem.at[1, 1])
    for p in range(n_seq):
        r, c = (p // s_across) * sr, (p % s_across) * sc
        up_out[r : r + sr, c : c + sc] = seq_all[1, p]

    kv_copies[0].wait_send()
    kv_copies[1].wait_send()
    back_pair_copy.wait_send()
    for n in range(1, n_block + 1):
        pairs[n].wait_send()
        settle(act_send.at[n - 1, pl.ds(0, n_chip - 1)], rs_send_sem.at[n - 1])
    settle(back_send.at[pl.ds(0, n_chip - 1)], rs_send_sem.at[n_block])
    settle(act_all.at[0, pl.ds(0, n_head - 1)], ag_send_sem.at[0])
    settle(act_all.at[1, pl.ds(0, n_head - 1)], ag_send_sem.at[1])
    settle(back_all.at[pl.ds(0, n_head - 1)], ag_send_sem.at[2])
    for kind in range(2):
        settle(seq_send.at[kind, pl.ds(0, n_seq - 1)], seq_send_sem.at[kind, 0])
        settle(seq_all.at[kind, pl.ds(0, n_seq - 1)], seq_send_sem.at[kind, 1])

    @pl.when(sh == 1)
    def _():
        for copy in tails + forwards:
            copy.wait_send()


def solution(mesh):
    n_seq, n_head = mesh.shape["seq"], mesh.shape["head"]
    n_chip = n_head // 2
    in_specs = (
        P("seq", "head"),
        P("head", "seq"),
        P("head", "seq"),
        P("head", None),
        P(None, "head"),
        P("seq", "head"),
    )
    out_specs = (P(None, "seq"), P("head", None), P(None, "head"))

    def on_device(queries, keys, values, down_factor, up_factor, gradient):
        length, width = queries.shape
        own = keys.shape[0]
        rank = up_factor.shape[0]
        n_block = length // block
        joined = length + length // 2
        pr, pc, _ = pieces_of(rank // 2, block, n_chip)
        sr, sc, _ = pieces_of(rank, block, n_seq)
        f32, b16 = jnp.float32, jnp.bfloat16
        dma = pltpu.SemaphoreType.DMA
        anywhere = pl.BlockSpec(memory_space=pl.ANY)
        vmem = pl.BlockSpec(memory_space=pltpu.VMEM)
        return pl.pallas_call(
            functools.partial(kernel, n_seq, n_head),
            out_shape=(
                jax.ShapeDtypeStruct((rank, length), f32),
                jax.ShapeDtypeStruct((width, rank), f32),
                jax.ShapeDtypeStruct((rank, width), f32),
            ),
            in_specs=[anywhere, anywhere, anywhere, vmem, vmem, anywhere],
            out_specs=(vmem, vmem, vmem),
            scratch_shapes=[
                pltpu.VMEM((length, width), b16),
                pltpu.VMEM((length, width), b16),
                pltpu.VMEM((2 * own, joined), b16),
                pltpu.VMEM((2 * own, joined), b16),
                pltpu.VMEM((joined, 2 * own), b16),
                pltpu.VMEM((width, length), b16),
                pltpu.VMEM((2, n_block, rank // 2, block), f32),
                pltpu.VMEM((n_block, rank // 2, block), f32),
                pltpu.VMEM((n_chip, n_block, pr, pc), sum_type),
                pltpu.VMEM((n_chip, n_block, pr, pc), sum_type),
                pltpu.VMEM((n_head, n_block, pr, pc), b16),
                pltpu.VMEM((rank, length), b16),
                pltpu.VMEM((n_block, 2, rank // 2, block), f32),
                pltpu.VMEM((n_block, rank // 2, block), f32),
                pltpu.VMEM((n_block, n_chip, pr, pc), sum_type),
                pltpu.VMEM((n_block, n_chip, pr, pc), sum_type),
                pltpu.VMEM((2, n_head, n_block // 2, pr, pc), b16),
                pltpu.VMEM((rank, length), b16),
                pltpu.VMEM((2, n_seq, sr, sc), f32),
                pltpu.VMEM((2, n_seq, sr, sc), f32),
                pltpu.VMEM((2, n_seq, sr, sc), f32),
                dma((4,)),
                dma((6,)),
                dma((6,)),
                dma((n_block + 1,)),
                dma((n_block + 1,)),
                dma((n_block + 1,)),
                dma((n_block + 1,)),
                dma((3,)),
                dma((3,)),
                dma((2, 2)),
                dma((2, 2)),
            ],
            compiler_params=pltpu.CompilerParams(
                collective_id=0, has_side_effects=True, vmem_limit_bytes=56 * 2**20
            ),
            cost_estimate=pl.CostEstimate(
                flops=6 * 10**9, bytes_accessed=8 * 2**20, transcendentals=10**7
            ),
        )(queries, keys, values, down_factor, up_factor, gradient)

    return jax.shard_map(
        on_device, mesh=mesh, in_specs=in_specs, out_specs=out_specs, check_vma=False
    )
```

profile of v0, /device:TPU:0, one launch (start us, length us, event | category | flops | bytes accessed | tf_op | source)
XLA Modules:
  0.0 59.5 jit_solution(5923692297266490559)
XLA Ops:
  0.6 1.6 %copy.9.down_ref = bf16[512,64]{1,0:T(8,128)(2,1)} copy(bf16[512,64]{0,1:T(8,128)(2,1)} %param.9) | data formatting | bytes 131072 | tf_op args[3]
  2.2 52.1 %shard_map.85 = (f32[64,2048]{1,0:T(8,128)}, f32[512,64]{1,0:T(8,128)}, f32[64,512]{1,0:T(8,128)}) custom-call(bf16[2048,512]{1,0:T(8,128)(2,1)} %q_hbm.1, bf16[64,2048]{1,0:T(8,128)(2,1)} %k_hbm.1, bf16[64,2048]{1,0:T(8,128)(2,1)} %v_hbm.1, bf16[512,64]{1,0:T(8,128)(2,1)} %copy.9.down_ref, bf16[64,512]{1,0:T(8,128)(2,1)} %up_ref.1, bf16[2048,512]{1,0:T(8,128)(2,1)} %grad_hbm.1), custom_call_target="tpu_custom_call" | custom-call | flops 6000000000 | bytes 8388608 | tf_op jit(solution)/shard_map/pallas_call | solution.py:485
  54.4 1.7 %copy.10 = f32[512,64]{0,1:T(8,128)} copy(f32[512,64]{1,0:T(8,128)} %get-tuple-element.4) | data formatting | bytes 262144 | tf_op jit(solution)/shard_map/pallas_call | solution.py:485
  56.1 1.9 %copy.13 = f32[64,2048]{1,0:T(8,128)} copy(f32[64,2048]{1,0:T(8,128)} %get-tuple-element.9) | data formatting | bytes 1048576
  57.9 1.6 %copy.14 = f32[64,512]{1,0:T(8,128)} copy(f32[64,512]{1,0:T(8,128)} %get-tuple-element.11) | data formatting | bytes 262144
where the time goes:
time: 59.8 us; the launch traced here: 59.5 us
  Pallas kernels  52.1 us (87%)
  local copies, waits for them, and re-layouts  6.76 us (11%)
  between operations  0.64 us (1%)
    pallas_call x1, Pallas kernels, on_device(): pl.pallas_call(functools.partial(kernel, n_seq, n_head), out_shape=(jax.S...  52.1 us
    unnamed x3, local copies, waits for them, and re-layouts  5.04 us
    pallas_call x1, local copies, waits for them, and re-layouts, on_device(): pl.pallas_call(functools.partial(kernel, n_seq, n_head), out_shape=(jax.S...  1.72 us

commit v1 on v0

--- a/solution.py
+++ b/solution.py
@@ -14,7 +14,6 @@
 block = 512
 sum_type = jnp.bfloat16
 NT = (((1,), (1,)), ((), ()))
-TN = (((0,), (0,)), ((), ()))
 
 
 def pieces_of(rows, columns, count):
@@ -32,14 +31,14 @@
     down_ref,
     up_ref,
     grad_hbm,
-    act_out,
+    low_ref,
     down_out,
     up_out,
     q_ref,
     grad_ref,
     k_ref,
     v_ref,
-    kt_ref,
+    vt_ref,
     attn_ref,
     back_pair,
     back_pair_in,
@@ -52,7 +51,6 @@
     act_send,
     act_in,
     act_all,
-    low_ref,
     seq_send,
     seq_in,
     seq_all,
@@ -191,7 +189,7 @@
     kv_copies[0].wait_recv()
     kv_copies[1].wait_recv()
     for c in range(half, half + length, block):
-        kt_ref[c : c + block, :] = k_ref[:, c : c + block].T
+        vt_ref[c : c + block, :] = v_ref[:, c : c + block].T
 
     def peers():
         for step in range(1, n_chip):
@@ -248,9 +246,9 @@
 
     def act_part(n):
         b = block_of(n)
-        columns = pl.ds(pl.multiple_of(b * block, block), block)
+        rows = pl.ds(pl.multiple_of(b * block, block), block)
         part = lax.dot_general(
-            down_ref[...], attn_ref[:, columns], TN, preferred_element_type=jnp.float32
+            down_ref[...], attn_ref[rows, :], NT, preferred_element_type=jnp.float32
         )
         act_pair[n - 1, 0] = part[:mid]
         act_pair[n - 1, 1] = part[mid:]
@@ -294,7 +292,6 @@
             for i, b in enumerate(range(odd, n_block, 2)):
                 value = act_all[odd, d, i]
                 low_ref[r : r + pr, b * block + c : b * block + c + pc] = value
-                act_out[r : r + pr, b * block + c : b * block + c + pc] = value.astype(jnp.float32)
 
     def up_part(odd):
         total = None
@@ -321,31 +318,26 @@
             columns = pl.ds(pl.multiple_of(h * head_size, head_size), head_size)
             for r in range(2):
                 rows = pl.ds(pl.multiple_of(b * block + r * sub, sub), sub)
-                query = q_ref[rows, columns]
-                count = (n - 1) * 2 + r + 1
-                scores = []
-                for j in range(count):
-                    keys = kt_ref[pl.ds(pl.multiple_of(start + j * sub, sub), sub), :]
-                    score = lax.dot_general(keys, query, NT, preferred_element_type=jnp.float32)
-                    if j == count - 1:
-                        key_index = lax.broadcasted_iota(jnp.int32, score.shape, 0)
-                        row_index = lax.broadcasted_iota(jnp.int32, score.shape, 1)
-                        score = jnp.where(key_index <= row_index, score, neg_big)
-                    scores.append(score)
-                top = jnp.max(scores[0], axis=0, keepdims=True)
-                for score in scores[1:]:
-                    top = jnp.maximum(top, jnp.max(score, axis=0, keepdims=True))
-                total, context = None, None
-                for j in range(count):
-                    weights = jnp.exp2((scores[j] - top) * factor)
-                    row_sum = jnp.sum(weights, axis=0, keepdims=True)
-                    values = v_ref[:, pl.ds(pl.multiple_of(start + j * sub, sub), sub)]
-                    term = jnp.dot(
-                        values, weights.astype(jnp.bfloat16), preferred_element_type=jnp.float32
-                    )
-                    total = row_sum if total is None else total + row_sum
-                    context = term if context is None else context + term
-                attn_ref[columns, rows] = (context * (1.0 / total)).astype(jnp.bfloat16)
+                count = ((n - 1) * 2 + r + 1) * sub
+                keys = pl.ds(start, count)
+                scores = jnp.dot(
+                    q_ref[rows, columns], k_ref[:, keys], preferred_element_type=jnp.float32
+                )
+                last = scores[:, count - sub :]
+                row_index = lax.broadcasted_iota(jnp.int32, last.shape, 0)
+                key_index = lax.broadcasted_iota(jnp.int32, last.shape, 1)
+                last = jnp.where(key_index <= row_index, last, neg_big)
+                if count > sub:
+                    scores = jnp.concatenate([scores[:, : count - sub], last], axis=1)
+                else:
+                    scores = last
+                top = jnp.max(scores, axis=1, keepdims=True)
+                weights = jnp.exp2((scores - top) * factor)
+                total = jnp.sum(weights, axis=1, keepdims=True)
+                context = jnp.dot(
+                    weights.astype(jnp.bfloat16), vt_ref[keys, :], preferred_element_type=jnp.float32
+                )
+                attn_ref[rows, columns] = (context * (1.0 / total)).astype(jnp.bfloat16)
             return carry
 
         lax.fori_loop(0, n_local, body, 0)
@@ -368,7 +360,7 @@
         for copy in forwards:
             copy.wait_recv()
         for c in range(0, half, block):
-            kt_ref[c : c + block, :] = k_ref[:, c : c + block].T
+            vt_ref[c : c + block, :] = v_ref[:, c : c + block].T
 
     def early():
         act_scatter(2, pairs[2])
@@ -420,7 +412,7 @@
     act_scatter(3, pairs[3])
     seq_scatter(
         0,
-        lax.dot_general(back_ref[...], attn_ref[...], NT, preferred_element_type=jnp.float32),
+        jnp.dot(back_ref[...], attn_ref[...], preferred_element_type=jnp.float32),
     )
     act_gather(0)
     seq_gather(0)
@@ -430,7 +422,7 @@
     settle(seq_all.at[0, pl.ds(0, n_seq - 1)], seq_in_sem.at[0, 1])
     for p in range(n_seq):
         r, c = (p // s_across) * sr, (p % s_across) * sc
-        down_out[c : c + sc, r : r + sr] = seq_all[0, p].T
+        down_out[r : r + sr, c : c + sc] = seq_all[0, p]
     seq_gather(1)
     settle(seq_all.at[1, pl.ds(0, n_seq - 1)], seq_in_sem.at[1, 1])
     for p in range(n_seq):
@@ -457,6 +449,12 @@
             copy.wait_send()
 
 
+def finish(low_ref, down_ref, up_ref, act_out, down_out, up_out):
+    act_out[...] = low_ref[...].astype(jnp.float32)
+    down_out[...] = down_ref[...]
+    up_out[...] = up_ref[...]
+
+
 def solution(mesh):
     n_seq, n_head = mesh.shape["seq"], mesh.shape["head"]
     n_chip = n_head // 2
@@ -482,11 +480,11 @@
         dma = pltpu.SemaphoreType.DMA
         anywhere = pl.BlockSpec(memory_space=pl.ANY)
         vmem = pl.BlockSpec(memory_space=pltpu.VMEM)
-        return pl.pallas_call(
+        low, down, up = pl.pallas_call(
             functools.partial(kernel, n_seq, n_head),
             out_shape=(
-                jax.ShapeDtypeStruct((rank, length), f32),
-                jax.ShapeDtypeStruct((width, rank), f32),
+                jax.ShapeDtypeStruct((rank, length), b16),
+                jax.ShapeDtypeStruct((rank, width), f32),
                 jax.ShapeDtypeStruct((rank, width), f32),
             ),
             in_specs=[anywhere, anywhere, anywhere, vmem, vmem, anywhere],
@@ -497,7 +495,7 @@
                 pltpu.VMEM((2 * own, joined), b16),
                 pltpu.VMEM((2 * own, joined), b16),
                 pltpu.VMEM((joined, 2 * own), b16),
-                pltpu.VMEM((width, length), b16),
+                pltpu.VMEM((length, width), b16),
                 pltpu.VMEM((2, n_block, rank // 2, block), f32),
                 pltpu.VMEM((n_block, rank // 2, block), f32),
                 pltpu.VMEM((n_chip, n_block, pr, pc), sum_type),
@@ -509,7 +507,6 @@
                 pltpu.VMEM((n_block, n_chip, pr, pc), sum_type),
                 pltpu.VMEM((n_block, n_chip, pr, pc), sum_type),
                 pltpu.VMEM((2, n_head, n_block // 2, pr, pc), b16),
-                pltpu.VMEM((rank, length), b16),
                 pltpu.VMEM((2, n_seq, sr, sc), f32),
                 pltpu.VMEM((2, n_seq, sr, sc), f32),
                 pltpu.VMEM((2, n_seq, sr, sc), f32),
@@ -531,7 +528,18 @@
             cost_estimate=pl.CostEstimate(
                 flops=6 * 10**9, bytes_accessed=8 * 2**20, transcendentals=10**7
             ),
-        )(queries, keys, values, down_factor, up_factor, gradient)
+        )(queries, keys, values, down_factor.T, up_factor, gradient)
+        activations, down, up = pl.pallas_call(
+            finish,
+            out_shape=(
+                jax.ShapeDtypeStruct((rank, length), f32),
+                jax.ShapeDtypeStruct((rank, width), f32),
+                jax.ShapeDtypeStruct((rank, width), f32),
+            ),
+            in_specs=[vmem, vmem, vmem],
+            out_specs=(vmem, vmem, vmem),
+        )(low, down, up)
+        return activations, down.T, up
 
     return jax.shard_map(
         on_device, mesh=mesh, in_specs=in_specs, out_specs=out_specs, check_vma=False

time: 59.8 us -> 54.5 us (0.911)
  local copies, waits for them, and re-layouts: 6.76 us -> 0 us
  Pallas kernels: 52.1 us -> 53.6 us
    unnamed x3 -> x0, local copies, waits for them, and re-layouts: 5.04 us -> none
    pallas_call x0 -> x1, Pallas kernels: none -> 1.94 us  [on_device(): pl.pallas_call(finish, out_shape=(jax.ShapeDtypeStruct((rank, length), f3...]
    pallas_call x1 -> x0, local copies, waits for them, and re-layouts: 1.72 us -> none  [on_device(): pl.pallas_call(functools.partial(kernel, n_seq, n_head), out_shape=(jax.S...]
where the time goes in v1:
time: 54.5 us; the launch traced here: 54.3 us
  Pallas kernels  53.6 us (98%)
  between operations  0.64 us (1%)
    pallas_call x1, Pallas kernels, on_device(): pl.pallas_call(functools.partial(kernel, n_seq, n_head), out_shape=(jax.S...  51.7 us
    pallas_call x1, Pallas kernels, on_device(): pl.pallas_call(finish, out_shape=(jax.ShapeDtypeStruct((rank, length), f3...  1.94 us

profile of v1, /device:TPU:0, one launch (start us, length us, event | category | flops | bytes accessed | tf_op | source)
XLA Modules:
  0.0 54.3 jit_solution(8066234153912507106)
XLA Ops:
  0.6 51.7 %shard_map.85 = (bf16[64,2048]{1,0:T(8,128)(2,1)}, f32[64,512]{1,0:T(8,128)}, f32[64,512]{1,0:T(8,128)}) custom-call(bf16[2048,512]{1,0:T(8,128)(2,1)} %q_hbm.1, bf16[64,2048]{1,0:T(8,128)(2,1)} %k_hbm.1, bf16[64,2048]{1,0:T(8,128)(2,1)} %v_hbm.1, bf16[64,512]{1,0:T(8,128)(2,1)} %bitcast.3, bf16[64,512]{1,0:T(8,128)(2,1)} %up_ref.1, bf16[2048,512]{1,0:T(8,128)(2,1)} %grad_hbm.1), custom_call_target="tpu_custom_call" | custom-call | flops 6000000000 | bytes 8388608 | tf_op jit(solution)/shard_map/pallas_call | solution.py:483
  52.3 1.9 %shard_map.86 = (f32[64,2048]{1,0:T(8,128)}, f32[64,512]{1,0:T(8,128)}, f32[64,512]{1,0:T(8,128)}) custom-call(bf16[64,2048]{1,0:T(8,128)(2,1)} %get-tuple-element.9.low_ref, f32[64,512]{1,0:T(8,128)} %get-tuple-element.10.down_ref, f32[64,512]{1,0:T(8,128)} %get-tuple-element.11.up_ref), custom_call_target="tpu_custom_call" | custom-call | tf_op jit(solution)/shard_map/pallas_call | solution.py:532

commit v2 on v1

--- a/solution.py
+++ b/solution.py
@@ -51,6 +51,10 @@
     act_send,
     act_in,
     act_all,
+    last_send,
+    last_in,
+    s0_ref,
+    s1_ref,
     seq_send,
     seq_in,
     seq_all,
@@ -124,16 +128,6 @@
     for copy in (grad_copy, k_copy, v_copy, q_copy):
         copy.start()
 
-    grad_copy.wait()
-    for b in range(n_block):
-        part = lax.dot_general(
-            up_ref[...],
-            grad_ref[b * block : (b + 1) * block, :],
-            NT,
-            preferred_element_type=jnp.float32,
-        )
-        back_pair[0, b] = part[:mid]
-        back_pair[1, b] = part[mid:]
     pl.semaphore_wait(barrier, n_head + n_seq - 2)
 
     kv_copies = []
@@ -176,6 +170,16 @@
         for copy in tails:
             copy.start()
 
+    grad_copy.wait()
+    for b in range(n_block):
+        part = lax.dot_general(
+            up_ref[...],
+            grad_ref[b * block : (b + 1) * block, :],
+            NT,
+            preferred_element_type=jnp.float32,
+        )
+        back_pair[0, b] = part[:mid]
+        back_pair[1, b] = part[mid:]
     back_pair_copy = remote(
         back_pair.at[1 - core],
         back_pair_in,
@@ -244,12 +248,14 @@
     def block_of(n):
         return lax.rem(n - 1 + sh * (n_block // 2), n_block)
 
+    def act_product(n):
+        rows = pl.ds(pl.multiple_of(block_of(n) * block, block), block)
+        return lax.dot_general(
+            down_ref[...], attn_ref[rows, :], NT, preferred_element_type=jnp.float32
+        )
+
     def act_part(n):
-        b = block_of(n)
-        rows = pl.ds(pl.multiple_of(b * block, block), block)
-        part = lax.dot_general(
-            down_ref[...], attn_ref[rows, :], NT, preferred_element_type=jnp.float32
-        )
+        part = act_product(n)
         act_pair[n - 1, 0] = part[:mid]
         act_pair[n - 1, 1] = part[mid:]
         return remote(
@@ -261,27 +267,50 @@
         )
 
     def act_scatter(n, copy):
-        b = block_of(n)
         copy.wait_recv()
         total = act_pair[n - 1, core] + act_pair_in[n - 1]
         for p in range(n_chip):
             act_send[n - 1, p] = piece(total, p).astype(sum_type)
-        act_in[b, chip] = act_send[n - 1, chip]
+        act_in[n - 1, chip] = act_send[n - 1, chip]
         for peer in peers():
             remote(
                 act_send.at[n - 1, peer],
-                act_in.at[b, chip],
+                act_in.at[n - 1, chip],
                 rs_send_sem.at[n - 1],
-                rs_in_sem.at[b],
+                rs_in_sem.at[n - 1],
                 {"head": peer * 2 + core},
             )
+
+    def last_scatter(n):
+        part = act_product(n)
+        for d in range(n_head):
+            r, c = place(d)
+            last_send[d] = part[r : r + pr, c : c + pc].astype(sum_type)
+        last_in[me_h] = last_send[me_h]
+        for step in range(1, n_head):
+            peer = lax.rem(me_h + step, n_head)
+            remote(
+                last_send.at[peer],
+                last_in.at[me_h],
+                rs_send_sem.at[n - 1],
+                rs_in_sem.at[n - 1],
+                {"head": peer},
+            )
+
+    last_step = n_block - 1
 
     def act_gather(odd):
         for i, b in enumerate(range(odd, n_block, 2)):
-            settle(act_in.at[b, pl.ds(0, n_chip - 1)], rs_in_sem.at[b])
-            total = act_in[b, 0].astype(jnp.float32)
-            for p in range(1, n_chip):
-                total = total + act_in[b, p].astype(jnp.float32)
+            total = None
+            for p in range(n_chip):
+                n = b + 1 if p >= n_chip // 2 else (b + n_block // 2) % n_block + 1
+                if n == last_step:
+                    terms = [last_in[2 * p], last_in[2 * p + 1]]
+                else:
+                    terms = [act_in[n - 1, p]]
+                for term in terms:
+                    term = term.astype(jnp.float32)
+                    total = term if total is None else total + term
             act_all[odd, me_h, i] = total.astype(jnp.bfloat16)
         gather_send(act_all.at[odd], odd)
 
@@ -312,35 +341,70 @@
         shifted_start = length if n <= n_block // 2 else 0
         start = pl.multiple_of(half + sh * (shifted_start - half), half)
 
-        def body(h, carry):
+        counts = (2 * n - 1, 2 * n)
+        strips = (s0_ref, s1_ref)
+
+        def rows_of(r):
+            return pl.ds(pl.multiple_of(b * block + r * sub, sub), sub)
+
+        def columns_of(h):
+            return pl.ds(pl.multiple_of(h * head_size, head_size), head_size)
+
+        def keys_of(j):
+            return pl.ds(pl.multiple_of(start + j * sub, sub), sub)
+
+        def score(r, h, j, top):
+            value = jnp.dot(
+                q_ref[rows_of(r), columns_of(h)],
+                k_ref[:, keys_of(j)],
+                preferred_element_type=jnp.float32,
+            )
+            if j == counts[r] - 1:
+                row_index = lax.broadcasted_iota(jnp.int32, value.shape, 0)
+                key_index = lax.broadcasted_iota(jnp.int32, value.shape, 1)
+                value = jnp.where(key_index <= row_index, value, neg_big)
+            strips[r][:, j * sub : (j + 1) * sub] = value
+            for c in range(0, sub, 128):
+                part = value[:, c : c + 128]
+                top = part if top is None else jnp.maximum(top, part)
+            return top
+
+        def weigh(r, j, top, state):
+            weights = jnp.exp2((strips[r][:, j * sub : (j + 1) * sub] - top) * factor)
+            total, context = state
+            for c in range(0, sub, 128):
+                part = weights[:, c : c + 128]
+                total = part if total is None else total + part
+            term = jnp.dot(
+                weights.astype(jnp.bfloat16),
+                vt_ref[keys_of(j), :],
+                preferred_element_type=jnp.float32,
+            )
+            return total, term if context is None else context + term
+
+        def phase(r, h, top, next_r, next_h):
+            top = jnp.max(top, axis=1, keepdims=True)
+            state, next_top = (None, None), None
+            for j in range(2 * n):
+                if j < counts[next_r]:
+                    next_top = score(next_r, next_h, j, next_top)
+                if j < counts[r]:
+                    state = weigh(r, j, top, state)
+            total, context = state
+            total = jnp.sum(total, axis=1, keepdims=True)
+            attn_ref[rows_of(r), columns_of(h)] = (context * (1.0 / total)).astype(jnp.bfloat16)
+            return next_top
+
+        def body(h, top):
             for at, hook in hooks:
                 pl.when(h == at)(hook)
-            columns = pl.ds(pl.multiple_of(h * head_size, head_size), head_size)
-            for r in range(2):
-                rows = pl.ds(pl.multiple_of(b * block + r * sub, sub), sub)
-                count = ((n - 1) * 2 + r + 1) * sub
-                keys = pl.ds(start, count)
-                scores = jnp.dot(
-                    q_ref[rows, columns], k_ref[:, keys], preferred_element_type=jnp.float32
-                )
-                last = scores[:, count - sub :]
-                row_index = lax.broadcasted_iota(jnp.int32, last.shape, 0)
-                key_index = lax.broadcasted_iota(jnp.int32, last.shape, 1)
-                last = jnp.where(key_index <= row_index, last, neg_big)
-                if count > sub:
-                    scores = jnp.concatenate([scores[:, : count - sub], last], axis=1)
-                else:
-                    scores = last
-                top = jnp.max(scores, axis=1, keepdims=True)
-                weights = jnp.exp2((scores - top) * factor)
-                total = jnp.sum(weights, axis=1, keepdims=True)
-                context = jnp.dot(
-                    weights.astype(jnp.bfloat16), vt_ref[keys, :], preferred_element_type=jnp.float32
-                )
-                attn_ref[rows, columns] = (context * (1.0 / total)).astype(jnp.bfloat16)
-            return carry
-
-        lax.fori_loop(0, n_local, body, 0)
+            top = phase(0, h, top, 1, h)
+            return phase(1, h, top, 0, jnp.minimum(h + 1, n_local - 1))
+
+        first = None
+        for j in range(counts[0]):
+            first = score(0, 0, j, first)
+        lax.fori_loop(0, n_local, body, first)
 
     pairs = {}
     attend(2, [(1, back_scatter)])
@@ -374,8 +438,13 @@
         act_scatter(4, pairs[4])
         back_finish()
 
-    attend(3, [(1, late), (3, functools.partial(act_gather, 1))])
-    pairs[3] = act_part(3)
+    def late_gather():
+        for n in (2, 4):
+            settle(act_in.at[n - 1, pl.ds(0, n_chip - 1)], rs_in_sem.at[n - 1])
+        act_gather(1)
+
+    attend(3, [(1, late), (3, late_gather)])
+    last_scatter(3)
 
     def seq_scatter(kind, value):
         for p in range(n_seq):
@@ -409,11 +478,12 @@
 
     act_finish(1)
     up_total = up_part(1)
-    act_scatter(3, pairs[3])
     seq_scatter(
         0,
         jnp.dot(back_ref[...], attn_ref[...], preferred_element_type=jnp.float32),
     )
+    settle(act_in.at[0, pl.ds(0, n_chip - 1)], rs_in_sem.at[0])
+    settle(last_in.at[pl.ds(0, n_head - 1)], rs_in_sem.at[last_step - 1])
     act_gather(0)
     seq_gather(0)
     act_finish(0)
@@ -432,7 +502,8 @@
     kv_copies[0].wait_send()
     kv_copies[1].wait_send()
     back_pair_copy.wait_send()
-    for n in range(1, n_block + 1):
+    settle(last_send.at[pl.ds(0, n_head - 1)], rs_send_sem.at[last_step - 1])
+    for n in pairs:
         pairs[n].wait_send()
         settle(act_send.at[n - 1, pl.ds(0, n_chip - 1)], rs_send_sem.at[n - 1])
     settle(back_send.at[pl.ds(0, n_chip - 1)], rs_send_sem.at[n_block])
@@ -507,6 +578,10 @@
                 pltpu.VMEM((n_block, n_chip, pr, pc), sum_type),
                 pltpu.VMEM((n_block, n_chip, pr, pc), sum_type),
                 pltpu.VMEM((2, n_head, n_block // 2, pr, pc), b16),
+                pltpu.VMEM((n_head, pr, pc), sum_type),
+                pltpu.VMEM((n_head, pr, pc), sum_type),
+                pltpu.VMEM((block // 2, length), f32),
+                pltpu.VMEM((block // 2, length), f32),
                 pltpu.VMEM((2, n_seq, sr, sc), f32),
                 pltpu.VMEM((2, n_seq, sr, sc), f32),
                 pltpu.VMEM((2, n_seq, sr, sc), f32),

time: 54.5 us -> 52 us (0.954)
  Pallas kernels: 53.6 us -> 51.2 us
    pallas_call x1, Pallas kernels: 51.7 us -> 49.2 us  [on_device(): pl.pallas_call(functools.partial(kernel, n_seq, n_head), out_shape=(jax.S...]
where the time goes in v2:
time: 52 us; the launch traced here: 51.8 us
  Pallas kernels  51.2 us (98%)
  between operations  0.64 us (1%)
    pallas_call x1, Pallas kernels, on_device(): pl.pallas_call(functools.partial(kernel, n_seq, n_head), out_shape=(jax.S...  49.2 us
    pallas_call x1, Pallas kernels, on_device(): pl.pallas_call(finish, out_shape=(jax.ShapeDtypeStruct((rank, length), f3...  1.94 us

profile of v2, /device:TPU:0, one launch (start us, length us, event | category | flops | bytes accessed | tf_op | source)
XLA Modules:
  0.0 51.8 jit_solution(4385713695000034203)
XLA Ops:
  0.6 49.2 %shard_map.85 = (bf16[64,2048]{1,0:T(8,128)(2,1)}, f32[64,512]{1,0:T(8,128)}, f32[64,512]{1,0:T(8,128)}) custom-call(bf16[2048,512]{1,0:T(8,128)(2,1)} %q_hbm.1, bf16[64,2048]{1,0:T(8,128)(2,1)} %k_hbm.1, bf16[64,2048]{1,0:T(8,128)(2,1)} %v_hbm.1, bf16[64,512]{1,0:T(8,128)(2,1)} %bitcast.3, bf16[64,512]{1,0:T(8,128)(2,1)} %up_ref.1, bf16[2048,512]{1,0:T(8,128)(2,1)} %grad_hbm.1), custom_call_target="tpu_custom_call" | custom-call | flops 6000000000 | bytes 8388608 | tf_op jit(solution)/shard_map/pallas_call | solution.py:554
  49.9 1.9 %shard_map.86 = (f32[64,2048]{1,0:T(8,128)}, f32[64,512]{1,0:T(8,128)}, f32[64,512]{1,0:T(8,128)}) custom-call(bf16[64,2048]{1,0:T(8,128)(2,1)} %get-tuple-element.9.low_ref, f32[64,512]{1,0:T(8,128)} %get-tuple-element.10.down_ref, f32[64,512]{1,0:T(8,128)} %get-tuple-element.11.up_ref), custom_call_target="tpu_custom_call" | custom-call | tf_op jit(solution)/shard_map/pallas_call | solution.py:607

commit v3 on v2

--- a/solution.py
+++ b/solution.py
@@ -13,7 +13,6 @@
 head_size = 128
 block = 512
 sum_type = jnp.bfloat16
-NT = (((1,), (1,)), ((), ()))
 
 
 def pieces_of(rows, columns, count):
@@ -55,6 +54,9 @@
     last_in,
     s0_ref,
     s1_ref,
+    down_t,
+    up_send,
+    up_all,
     seq_send,
     seq_in,
     seq_all,
@@ -170,14 +172,12 @@
         for copy in tails:
             copy.start()
 
+    up_t = up_ref[...].T
     grad_copy.wait()
     for b in range(n_block):
-        part = lax.dot_general(
-            up_ref[...],
-            grad_ref[b * block : (b + 1) * block, :],
-            NT,
-            preferred_element_type=jnp.float32,
-        )
+        part = jnp.dot(
+            grad_ref[b * block : (b + 1) * block, :], up_t, preferred_element_type=jnp.float32
+        ).T
         back_pair[0, b] = part[:mid]
         back_pair[1, b] = part[mid:]
     back_pair_copy = remote(
@@ -188,6 +188,7 @@
         partner,
     )
 
+    down_t[...] = down_ref[...].T
     for copy in (k_copy, v_copy, q_copy):
         copy.wait()
     kv_copies[0].wait_recv()
@@ -250,9 +251,7 @@
 
     def act_product(n):
         rows = pl.ds(pl.multiple_of(block_of(n) * block, block), block)
-        return lax.dot_general(
-            down_ref[...], attn_ref[rows, :], NT, preferred_element_type=jnp.float32
-        )
+        return jnp.dot(attn_ref[rows, :], down_t[...], preferred_element_type=jnp.float32).T
 
     def act_part(n):
         part = act_product(n)
@@ -350,8 +349,8 @@
         def columns_of(h):
             return pl.ds(pl.multiple_of(h * head_size, head_size), head_size)
 
-        def keys_of(j):
-            return pl.ds(pl.multiple_of(start + j * sub, sub), sub)
+        def keys_of(j, wide=1):
+            return pl.ds(pl.multiple_of(start + j * sub, sub), wide * sub)
 
         def score(r, h, j, top):
             value = jnp.dot(
@@ -369,15 +368,15 @@
                 top = part if top is None else jnp.maximum(top, part)
             return top
 
-        def weigh(r, j, top, state):
-            weights = jnp.exp2((strips[r][:, j * sub : (j + 1) * sub] - top) * factor)
+        def weigh(r, j, wide, top, state):
+            weights = jnp.exp2((strips[r][:, j * sub : (j + wide) * sub] - top) * factor)
             total, context = state
-            for c in range(0, sub, 128):
+            for c in range(0, wide * sub, 128):
                 part = weights[:, c : c + 128]
                 total = part if total is None else total + part
             term = jnp.dot(
                 weights.astype(jnp.bfloat16),
-                vt_ref[keys_of(j), :],
+                vt_ref[keys_of(j, wide), :],
                 preferred_element_type=jnp.float32,
             )
             return total, term if context is None else context + term
@@ -388,8 +387,8 @@
             for j in range(2 * n):
                 if j < counts[next_r]:
                     next_top = score(next_r, next_h, j, next_top)
-                if j < counts[r]:
-                    state = weigh(r, j, top, state)
+                if j % 2 == 0 and j < counts[r]:
+                    state = weigh(r, j, min(2, counts[r] - j), top, state)
             total, context = state
             total = jnp.sum(total, axis=1, keepdims=True)
             attn_ref[rows_of(r), columns_of(h)] = (context * (1.0 / total)).astype(jnp.bfloat16)
@@ -446,58 +445,64 @@
     attend(3, [(1, late), (3, late_gather)])
     last_scatter(3)
 
-    def seq_scatter(kind, value):
+    def seq_scatter(value):
         for p in range(n_seq):
             r, c = (p // s_across) * sr, (p % s_across) * sc
-            seq_send[kind, p] = value[r : r + sr, c : c + sc]
-        seq_in[kind, me_s] = seq_send[kind, me_s]
+            seq_send[p] = value[r : r + sr, c : c + sc]
+        seq_in[me_s] = seq_send[me_s]
         for step in range(1, n_seq):
             peer = lax.rem(me_s + step, n_seq)
             remote(
-                seq_send.at[kind, peer],
-                seq_in.at[kind, me_s],
-                seq_send_sem.at[kind, 0],
-                seq_in_sem.at[kind, 0],
+                seq_send.at[peer],
+                seq_in.at[me_s],
+                seq_send_sem.at[0, 0],
+                seq_in_sem.at[0, 0],
                 {"seq": peer},
             )
 
-    def seq_gather(kind):
-        settle(seq_in.at[kind, pl.ds(0, n_seq - 1)], seq_in_sem.at[kind, 0])
-        total = seq_in[kind, 0]
+    def seq_gather():
+        settle(seq_in.at[pl.ds(0, n_seq - 1)], seq_in_sem.at[0, 0])
+        total = seq_in[0]
         for p in range(1, n_seq):
-            total = total + seq_in[kind, p]
-        seq_all[kind, me_s] = total * adapter_scale
+            total = total + seq_in[p]
+        seq_all[me_s] = total * adapter_scale
         for step in range(1, n_seq):
             remote(
-                seq_all.at[kind, me_s],
-                seq_all.at[kind, me_s],
-                seq_send_sem.at[kind, 1],
-                seq_in_sem.at[kind, 1],
+                seq_all.at[me_s],
+                seq_all.at[me_s],
+                seq_send_sem.at[0, 1],
+                seq_in_sem.at[0, 1],
                 {"seq": lax.rem(me_s + step, n_seq)},
             )
 
     act_finish(1)
     up_total = up_part(1)
-    seq_scatter(
-        0,
-        jnp.dot(back_ref[...], attn_ref[...], preferred_element_type=jnp.float32),
-    )
+    seq_scatter(jnp.dot(back_ref[...], attn_ref[...], preferred_element_type=jnp.float32))
     settle(act_in.at[0, pl.ds(0, n_chip - 1)], rs_in_sem.at[0])
     settle(last_in.at[pl.ds(0, n_head - 1)], rs_in_sem.at[last_step - 1])
     act_gather(0)
-    seq_gather(0)
+    seq_gather()
     act_finish(0)
-    seq_scatter(1, up_total + up_part(0))
-
-    settle(seq_all.at[0, pl.ds(0, n_seq - 1)], seq_in_sem.at[0, 1])
+    up_send[...] = (up_total + up_part(0)).astype(sum_type)
+    for step in range(1, n_seq):
+        remote(
+            up_send,
+            up_all.at[me_s],
+            seq_send_sem.at[1, 0],
+            seq_in_sem.at[1, 0],
+            {"seq": lax.rem(me_s + step, n_seq)},
+        )
+    up_all[me_s] = up_send[...]
+
+    settle(seq_all.at[pl.ds(0, n_seq - 1)], seq_in_sem.at[0, 1])
     for p in range(n_seq):
         r, c = (p // s_across) * sr, (p % s_across) * sc
-        down_out[r : r + sr, c : c + sc] = seq_all[0, p]
-    seq_gather(1)
-    settle(seq_all.at[1, pl.ds(0, n_seq - 1)], seq_in_sem.at[1, 1])
-    for p in range(n_seq):
-        r, c = (p // s_across) * sr, (p % s_across) * sc
-        up_out[r : r + sr, c : c + sc] = seq_all[1, p]
+        down_out[r : r + sr, c : c + sc] = seq_all[p]
+    settle(up_all.at[pl.ds(0, n_seq - 1)], seq_in_sem.at[1, 0])
+    total = up_all[0].astype(jnp.float32)
+    for p in range(1, n_seq):
+        total = total + up_all[p].astype(jnp.float32)
+    up_out[...] = total * adapter_scale
 
     kv_copies[0].wait_send()
     kv_copies[1].wait_send()
@@ -510,9 +515,9 @@
     settle(act_all.at[0, pl.ds(0, n_head - 1)], ag_send_sem.at[0])
     settle(act_all.at[1, pl.ds(0, n_head - 1)], ag_send_sem.at[1])
     settle(back_all.at[pl.ds(0, n_head - 1)], ag_send_sem.at[2])
-    for kind in range(2):
-        settle(seq_send.at[kind, pl.ds(0, n_seq - 1)], seq_send_sem.at[kind, 0])
-        settle(seq_all.at[kind, pl.ds(0, n_seq - 1)], seq_send_sem.at[kind, 1])
+    settle(seq_send.at[pl.ds(0, n_seq - 1)], seq_send_sem.at[0, 0])
+    settle(seq_all.at[pl.ds(0, n_seq - 1)], seq_send_sem.at[0, 1])
+    settle(up_all.at[pl.ds(0, n_seq - 1)], seq_send_sem.at[1, 0])
 
     @pl.when(sh == 1)
     def _():
@@ -582,9 +587,12 @@
                 pltpu.VMEM((n_head, pr, pc), sum_type),
                 pltpu.VMEM((block // 2, length), f32),
                 pltpu.VMEM((block // 2, length), f32),
-                pltpu.VMEM((2, n_seq, sr, sc), f32),
-                pltpu.VMEM((2, n_seq, sr, sc), f32),
-                pltpu.VMEM((2, n_seq, sr, sc), f32),
+                pltpu.VMEM((width, rank), b16),
+                pltpu.VMEM((rank, width), sum_type),
+                pltpu.VMEM((n_seq, rank, width), sum_type),
+                pltpu.VMEM((n_seq, sr, sc), f32),
+                pltpu.VMEM((n_seq, sr, sc), f32),
+                pltpu.VMEM((n_seq, sr, sc), f32),
                 dma((4,)),
                 dma((6,)),
                 dma((6,)),

time: 52 us -> 49.6 us (0.954)
  Pallas kernels: 51.2 us -> 48.8 us
    pallas_call x1, Pallas kernels: 49.2 us -> 46.8 us  [on_device(): pl.pallas_call(functools.partial(kernel, n_seq, n_head), out_shape=(jax.S...]
where the time goes in v3:
time: 49.6 us; the launch traced here: 49.4 us
  Pallas kernels  48.8 us (98%)
  between operations  0.64 us (1%)
    pallas_call x1, Pallas kernels, on_device(): pl.pallas_call(functools.partial(kernel, n_seq, n_head), out_shape=(jax.S...  46.8 us
    pallas_call x1, Pallas kernels, on_device(): pl.pallas_call(finish, out_shape=(jax.ShapeDtypeStruct((rank, length), f3...  1.94 us

profile of v3, /device:TPU:0, one launch (start us, length us, event | category | flops | bytes accessed | tf_op | source)
XLA Modules:
  0.0 49.4 jit_solution(12704648535751924879)
XLA Ops:
  0.6 46.8 %shard_map.85 = (bf16[64,2048]{1,0:T(8,128)(2,1)}, f32[64,512]{1,0:T(8,128)}, f32[64,512]{1,0:T(8,128)}) custom-call(bf16[2048,512]{1,0:T(8,128)(2,1)} %q_hbm.1, bf16[64,2048]{1,0:T(8,128)(2,1)} %k_hbm.1, bf16[64,2048]{1,0:T(8,128)(2,1)} %v_hbm.1, bf16[64,512]{1,0:T(8,128)(2,1)} %bitcast.3, bf16[64,512]{1,0:T(8,128)(2,1)} %up_ref.1, bf16[2048,512]{1,0:T(8,128)(2,1)} %grad_hbm.1), custom_call_target="tpu_custom_call" | custom-call | flops 6000000000 | bytes 8388608 | tf_op jit(solution)/shard_map/pallas_call | solution.py:559
  47.5 1.9 %shard_map.86 = (f32[64,2048]{1,0:T(8,128)}, f32[64,512]{1,0:T(8,128)}, f32[64,512]{1,0:T(8,128)}) custom-call(bf16[64,2048]{1,0:T(8,128)(2,1)} %get-tuple-element.9.low_ref, f32[64,512]{1,0:T(8,128)} %get-tuple-element.10.down_ref, f32[64,512]{1,0:T(8,128)} %get-tuple-element.11.up_ref), custom_call_target="tpu_custom_call" | custom-call | tf_op jit(solution)/shard_map/pallas_call | solution.py:615

commit v4 on v3

--- a/solution.py
+++ b/solution.py
@@ -30,9 +30,11 @@
     down_ref,
     up_ref,
     grad_hbm,
+    low_hbm,
+    down_hbm,
+    up_out,
     low_ref,
     down_out,
-    up_out,
     q_ref,
     grad_ref,
     k_ref,
@@ -189,12 +191,13 @@
     )
 
     down_t[...] = down_ref[...].T
+    vt_ref[:, head_size:] = jnp.ones((vt_ref.shape[0], head_size), jnp.bfloat16)
     for copy in (k_copy, v_copy, q_copy):
         copy.wait()
     kv_copies[0].wait_recv()
     kv_copies[1].wait_recv()
     for c in range(half, half + length, block):
-        vt_ref[c : c + block, :] = v_ref[:, c : c + block].T
+        vt_ref[c : c + block, :head_size] = v_ref[:, c : c + block].T
 
     def peers():
         for step in range(1, n_chip):
@@ -353,44 +356,41 @@
             return pl.ds(pl.multiple_of(start + j * sub, sub), wide * sub)
 
         def score(r, h, j, top):
+            wide = min(2, counts[r] - j)
             value = jnp.dot(
                 q_ref[rows_of(r), columns_of(h)],
-                k_ref[:, keys_of(j)],
+                k_ref[:, keys_of(j, wide)],
                 preferred_element_type=jnp.float32,
             )
-            if j == counts[r] - 1:
-                row_index = lax.broadcasted_iota(jnp.int32, value.shape, 0)
-                key_index = lax.broadcasted_iota(jnp.int32, value.shape, 1)
-                value = jnp.where(key_index <= row_index, value, neg_big)
-            strips[r][:, j * sub : (j + 1) * sub] = value
-            for c in range(0, sub, 128):
-                part = value[:, c : c + 128]
-                top = part if top is None else jnp.maximum(top, part)
+            for i in range(wide):
+                part = value[:, i * sub : (i + 1) * sub]
+                if j + i == counts[r] - 1:
+                    row_index = lax.broadcasted_iota(jnp.int32, part.shape, 0)
+                    key_index = lax.broadcasted_iota(jnp.int32, part.shape, 1)
+                    part = jnp.where(key_index <= row_index, part, neg_big)
+                strips[r][:, (j + i) * sub : (j + i + 1) * sub] = part
+                for c in range(0, sub, 128):
+                    lanes = part[:, c : c + 128]
+                    top = lanes if top is None else jnp.maximum(top, lanes)
             return top
 
         def weigh(r, j, wide, top, state):
             weights = jnp.exp2((strips[r][:, j * sub : (j + wide) * sub] - top) * factor)
-            total, context = state
-            for c in range(0, wide * sub, 128):
-                part = weights[:, c : c + 128]
-                total = part if total is None else total + part
             term = jnp.dot(
                 weights.astype(jnp.bfloat16),
                 vt_ref[keys_of(j, wide), :],
                 preferred_element_type=jnp.float32,
             )
-            return total, term if context is None else context + term
+            return term if state is None else state + term
 
         def phase(r, h, top, next_r, next_h):
             top = jnp.max(top, axis=1, keepdims=True)
-            state, next_top = (None, None), None
-            for j in range(2 * n):
-                if j < counts[next_r]:
-                    next_top = score(next_r, next_h, j, next_top)
-                if j % 2 == 0 and j < counts[r]:
+            state, next_top = None, None
+            for j in range(0, 2 * n, 2):
+                next_top = score(next_r, next_h, j, next_top)
+                if j < counts[r]:
                     state = weigh(r, j, min(2, counts[r] - j), top, state)
-            total, context = state
-            total = jnp.sum(total, axis=1, keepdims=True)
+            context, total = state[:, :head_size], state[:, head_size:]
             attn_ref[rows_of(r), columns_of(h)] = (context * (1.0 / total)).astype(jnp.bfloat16)
             return next_top
 
@@ -401,7 +401,7 @@
             return phase(1, h, top, 0, jnp.minimum(h + 1, n_local - 1))
 
         first = None
-        for j in range(counts[0]):
+        for j in range(0, counts[0], 2):
             first = score(0, 0, j, first)
         lax.fori_loop(0, n_local, body, first)
 
@@ -423,7 +423,7 @@
         for copy in forwards:
             copy.wait_recv()
         for c in range(0, half, block):
-            vt_ref[c : c + block, :] = v_ref[:, c : c + block].T
+            vt_ref[c : c + block, :head_size] = v_ref[:, c : c + block].T
 
     def early():
         act_scatter(2, pairs[2])
@@ -435,7 +435,6 @@
 
     def late():
         act_scatter(4, pairs[4])
-        back_finish()
 
     def late_gather():
         for n in (2, 4):
@@ -444,6 +443,7 @@
 
     attend(3, [(1, late), (3, late_gather)])
     last_scatter(3)
+    back_finish()
 
     def seq_scatter(value):
         for p in range(n_seq):
@@ -483,6 +483,8 @@
     act_gather(0)
     seq_gather()
     act_finish(0)
+    low_copy = pltpu.make_async_copy(low_ref, low_hbm, local_sem.at[4])
+    low_copy.start()
     up_send[...] = (up_total + up_part(0)).astype(sum_type)
     for step in range(1, n_seq):
         remote(
@@ -498,12 +500,17 @@
     for p in range(n_seq):
         r, c = (p // s_across) * sr, (p % s_across) * sc
         down_out[r : r + sr, c : c + sc] = seq_all[p]
+    down_copy = pltpu.make_async_copy(down_out, down_hbm, local_sem.at[5])
+    down_copy.start()
+
     settle(up_all.at[pl.ds(0, n_seq - 1)], seq_in_sem.at[1, 0])
     total = up_all[0].astype(jnp.float32)
     for p in range(1, n_seq):
         total = total + up_all[p].astype(jnp.float32)
     up_out[...] = total * adapter_scale
 
+    low_copy.wait()
+    down_copy.wait()
     kv_copies[0].wait_send()
     kv_copies[1].wait_send()
     back_pair_copy.wait_send()
@@ -564,13 +571,15 @@
                 jax.ShapeDtypeStruct((rank, width), f32),
             ),
             in_specs=[anywhere, anywhere, anywhere, vmem, vmem, anywhere],
-            out_specs=(vmem, vmem, vmem),
+            out_specs=(anywhere, anywhere, vmem),
             scratch_shapes=[
+                pltpu.VMEM((rank, length), b16),
+                pltpu.VMEM((rank, width), f32),
                 pltpu.VMEM((length, width), b16),
                 pltpu.VMEM((length, width), b16),
                 pltpu.VMEM((2 * own, joined), b16),
                 pltpu.VMEM((2 * own, joined), b16),
-                pltpu.VMEM((joined, 2 * own), b16),
+                pltpu.VMEM((joined, 4 * own), b16),
                 pltpu.VMEM((length, width), b16),
                 pltpu.VMEM((2, n_block, rank // 2, block), f32),
                 pltpu.VMEM((n_block, rank // 2, block), f32),
@@ -593,7 +602,7 @@
                 pltpu.VMEM((n_seq, sr, sc), f32),
                 pltpu.VMEM((n_seq, sr, sc), f32),
                 pltpu.VMEM((n_seq, sr, sc), f32),
-                dma((4,)),
+                dma((6,)),
                 dma((6,)),
                 dma((6,)),
                 dma((n_block + 1,)),

time: 49.6 us -> 47.4 us (0.956)
  Pallas kernels: 48.8 us -> 46.6 us
    pallas_call x1, Pallas kernels: 46.8 us -> 44.7 us  [on_device(): pl.pallas_call(functools.partial(kernel, n_seq, n_head), out_shape=(jax.S...]
where the time goes in v4:
time: 47.4 us; the launch traced here: 47.2 us
  Pallas kernels  46.6 us (98%)
  between operations  0.64 us (1%)
    pallas_call x1, Pallas kernels, on_device(): pl.pallas_call(functools.partial(kernel, n_seq, n_head), out_shape=(jax.S...  44.7 us
    pallas_call x1, Pallas kernels, on_device(): pl.pallas_call(finish, out_shape=(jax.ShapeDtypeStruct((rank, length), f3...  1.94 us

profile of v4, /device:TPU:0, one launch (start us, length us, event | category | flops | bytes accessed | tf_op | source)
XLA Modules:
  0.0 47.2 jit_solution(13599166147995423412)
XLA Ops:
  0.6 44.7 %shard_map.85 = (bf16[64,2048]{1,0:T(8,128)(2,1)}, f32[64,512]{1,0:T(8,128)}, f32[64,512]{1,0:T(8,128)}) custom-call(bf16[2048,512]{1,0:T(8,128)(2,1)} %q_hbm.1, bf16[64,2048]{1,0:T(8,128)(2,1)} %k_hbm.1, bf16[64,2048]{1,0:T(8,128)(2,1)} %v_hbm.1, bf16[64,512]{1,0:T(8,128)(2,1)} %bitcast.3, bf16[64,512]{1,0:T(8,128)(2,1)} %up_ref.1, bf16[2048,512]{1,0:T(8,128)(2,1)} %grad_hbm.1), custom_call_target="tpu_custom_call" | custom-call | flops 6000000000 | bytes 8388608 | tf_op jit(solution)/shard_map/pallas_call | solution.py:566
  45.3 1.9 %shard_map.86 = (f32[64,2048]{1,0:T(8,128)}, f32[64,512]{1,0:T(8,128)}, f32[64,512]{1,0:T(8,128)}) custom-call(bf16[64,2048]{1,0:T(8,128)(2,1)} %get-tuple-element.9.low_ref, f32[64,512]{1,0:T(8,128)} %get-tuple-element.10.down_ref, f32[64,512]{1,0:T(8,128)} %get-tuple-element.11.up_ref), custom_call_target="tpu_custom_call" | custom-call | tf_op jit(solution)/shard_map/pallas_call | solution.py:624
